TPU v7x, 256 devices: a whole 4x4x8 slice. The times are simulated.
256 devices in a mesh: row: 32 (over x, z_hi, core), col: 8 (over y, z_lo).
Axes of the slice: x: 4, y: 4, z: 8 (z_hi: 4, z_lo: 2; z = z_hi * 2 + z_lo), core: 2. Of those that a mesh axis runs over, the one named last changes fastest.
Arguments:
- activations: bfloat16 [1024, 18432], P('row', 'col'), may hold values from -6 to 6
- out_grads: bfloat16 [1024, 7168], P('col', 'row'), may hold values from -1 to 1
- query_acts: bfloat16 [64, 18432], P('row', 'col'), may hold values from -6 to 6
- query_grads: bfloat16 [64, 7168], P('col', 'row'), may hold values from -1 to 1
- basis_in: bfloat16 [18432, 18432], P('col', 'row'), may hold values from -0.046875 to 0.046875
- basis_out: bfloat16 [7168, 7168], P('row', 'col'), may hold values from -0.0625 to 0.0625
- damping: float32 [1], replicated, may hold values from 0.1 to 1
Outputs:
- corrected: float32 [7168, 18432], P('col', 'row')
All inputs are finite; a program needn't handle non-finite values.
Results may differ from a plain program's by a relative error of at most 0.0044.
Values may be sent and summed in bfloat16 or wider, within the bound.
No kernel may reach another device: no remote copies, remote signals or barrier semaphores. Data moves between devices by JAX's collectives and lax.ppermute only.
A program may use at most 64 MiB of HBM per device.

v0:
```python
import jax
import jax.numpy as jnp
from jax import lax
from jax.sharding import Mesh
from jax.sharding import PartitionSpec as P

TL = 64
EXAMPLES = 16
ROW = ("row_0", "row_1", "row_2")


def in_order(tiles, dim):
    tiles = jnp.moveaxis(tiles, 0, dim)
    shape = tiles.shape
    return tiles.reshape(*shape[:dim], shape[dim] * shape[dim + 1], *shape[dim + 2 :])


def copy_for_each(value, axis):
    peers = lax.axis_size(axis)
    return lax.all_to_all(
        jnp.broadcast_to(value[None], (peers, *value.shape)), axis, 0, 0, tiled=True
    )


def gathered_copies(value, axis, dim):
    return in_order(copy_for_each(value, axis), dim)


def in_blocks(value, dim, peers):
    shape = value.shape
    tiles = value.reshape(*shape[:dim], peers, shape[dim] // peers, *shape[dim + 1 :])
    return jnp.moveaxis(tiles, dim, 0)


def sent_and_summed(value, axis, dim):
    tiles = in_blocks(value, dim, lax.axis_size(axis))
    arrived = lax.all_to_all(tiles, axis, split_axis=0, concat_axis=0, tiled=True)
    return arrived.sum(axis=0)


def summed_rows(value, axes, dim):
    far, near = axes
    tiles = in_blocks(value, dim, lax.axis_size(far))
    nearer = sent_and_summed(tiles, near, dim + 1)
    arrived = lax.all_to_all(nearer, far, split_axis=0, concat_axis=0, tiled=True)
    return arrived.sum(axis=0)


def shards(activations, out_grads, query_acts, query_grads, basis_in, basis_out, damping):
    train_act = activations.shape[0]
    block_act = train_act + query_acts.shape[0]
    act_local = jnp.concatenate([activations, query_acts], 0)
    partial_in = jnp.dot(
        lax.all_gather(act_local, ROW, axis=0, tiled=True),
        basis_in,
        preferred_element_type=jnp.float32,
    )
    train_grad = out_grads.shape[0]
    block_grad = train_grad + query_grads.shape[0]
    grad_local = jnp.concatenate([out_grads, query_grads], 0)
    partial_out = jnp.dot(
        gathered_copies(grad_local, "col", 0), basis_out, preferred_element_type=jnp.float32
    )
    share_in = sent_and_summed(partial_in, "col", 0).astype(jnp.bfloat16)
    summed_in = gathered_copies(share_in, "col", 0)
    share_out = summed_rows(partial_out, (("row_0", "row_1"), "row_2"), 0).astype(jnp.bfloat16)
    summed_out = lax.all_gather(share_out, ROW, axis=0, tiled=True)
    width_in = summed_in.shape[1]
    width_out = summed_out.shape[1]
    groups_in = summed_in.reshape(lax.axis_size(ROW), block_act, width_in)
    rot_act = groups_in[:, :train_act].reshape(-1, width_in)
    q_act = groups_in[:, train_act:].reshape(-1, width_in)
    groups_out = summed_out.reshape(lax.axis_size("col"), block_grad, width_out)
    rot_grad = groups_out[:, :train_grad].reshape(-1, width_out)
    q_grad = groups_out[:, train_grad:].reshape(-1, width_out)

    def accumulate(index, total):
        act_block = lax.dynamic_slice_in_dim(rot_act, index * TL, TL, 0)
        grad_block = lax.dynamic_slice_in_dim(rot_grad, index * TL, TL, 0)
        outer = lax.dot_general(
            grad_block, act_block, (((0,), (0,)), ((), ())), preferred_element_type=jnp.float32
        )
        return total + outer * outer

    moment = (
        lax.fori_loop(0, EXAMPLES, accumulate, jnp.zeros((width_out, width_in), jnp.float32))
        / EXAMPLES
    )
    query = lax.dot_general(
        q_grad, q_act, (((0,), (0,)), ((), ())), preferred_element_type=jnp.float32
    )
    return query / (moment + damping[0])


def solution(mesh):
    finer = Mesh(
        mesh.devices.reshape(4, 4, 2, mesh.shape["col"]), ("row_0", "row_1", "row_2", "col")
    )
    placed = (
        P(ROW, "col"),
        P("col", ROW),
        P(ROW, "col"),
        P("col", ROW),
        P("col", ROW),
        P(ROW, "col"),
        P(),
    )
    return jax.shard_map(
        shards, mesh=finer, in_specs=placed, out_specs=P("col", ROW), check_vma=False
    )
```

profile of v0, /device:TPU:1, one launch (start us, length us, event | category | flops | bytes accessed | tf_op | source)
XLA Modules:
  0.0 283.4 jit_solution(13699588076466373404)
XLA Ops:
  6.5 0.0 copy-start
  6.5 0.0 all-gather.7.cloned.1.call-start
  6.5 1.8 maximum_bitcast_fusion
  8.3 0.0 all-gather.7.cloned.1.call-update
  8.3 0.8 copy.21
  9.2 0.8 pad_maximum_fusion
  10.0 0.1 copy.22
  10.2 15.6 %all_to_all.25 = bf16[8,136,224]{2,1,0:T(8,128)(2,1)} all-to-all(bf16[8,136,224]{2,1,0:T(8,128)(2,1)S(1)} %broadcast_in_dim.6), channel_id=1, replica_groups=mesh['row_0'=4,'row_1'=4,'row_2'=2,'col'=8] {'col'}, dimensions={0} | all-to-all | bytes 974848 | tf_op jit(solution)/shard_map/all_to_all | solution.py:20
  25.8 1.4 dot_general.18
  27.2 1.8 convolution_bitcast_fusion
  29.0 1.3 copy.23
  30.3 9.7 %all_to_all.26 = f32[2,16,34,896]{3,1,2,0:T(8,128)} all-to-all(f32[2,16,34,896]{3,1,2,0:T(8,128)S(1)} %copy.23), channel_id=1, replica_groups=mesh['row_0'=4,'row_1'=4,'row_2'=2,'col'=8] {'row_2'}, dimensions={0} | all-to-all | bytes 7798784 | tf_op jit(solution)/shard_map/all_to_all | solution.py:37
  40.0 3.8 %reduce_sum.27 = f32[16,34,896]{2,0,1:T(8,128)} reduce(f32[2,16,34,896]{3,1,2,0:T(8,128)} %all_to_all.26, f32[]{:T(128)} %constant.33.clone.1), dimensions={0}, to_apply=%region_0.0 | reduce | flops 487424 | bytes 5849092 | tf_op jit(solution)/shard_map/reduce_sum | solution.py:38
  43.9 3.5 %copy.24 = f32[16,34,896]{2,1,0:T(8,128)} copy(f32[16,34,896]{2,0,1:T(8,128)} %reduce_sum.27) | data formatting | bytes 3899392 | tf_op jit(solution)/shard_map/reduce_sum | solution.py:38
  47.4 9.9 %all-to-all-start.2 = ((f32[16,34,896]{2,1,0:T(8,128)}), f32[16,34,896]{2,1,0:T(8,128)}, u32[]{:S(2)}, u32[]{:S(2)}) async-start(f32[16,34,896]{2,1,0:T(8,128)} %copy.24), calls=%async_computation.2 | async-start | bytes 4587520 | tf_op jit(solution)/shard_map/all_to_all | solution.py:45
  57.3 53.6 %all-gather.7.cloned.1.call-done = bf16[32,34,2304]{2,1,0:T(8,128)(2,1)} async-done(((bf16[1,34,2304]{2,1,0:T(8,128)(2,1)}), bf16[32,34,2304]{2,1,0:T(8,128)(2,1)}) %all-gather.7.cloned.1.call-update) | async-done | bytes 5013520 | tf_op jit(solution)/shard_map/all_gather | solution.py:54
  110.9 7.8 %reshape.34 = bf16[1088,2304]{1,0:T(8,128)(2,1)} reshape(bf16[32,34,2304]{2,1,0:T(8,128)(2,1)} %all-gather.7.cloned.1.call-done) | data formatting | bytes 10027008
  118.7 0.0 copy-done
  118.7 8.1 %fusion.4 = f32[1088,576]{1,0:T(8,128)} fusion(bf16[1088,2304]{1,0:T(8,128)(2,1)} %reshape.34, bf16[2304,576]{0,1:T(8,128)(2,1)S(1)} %copy-done), kind=kOutput, calls=%fused_computation.11 | convolution fusion | flops 2887778304 | bytes 10174464 | tf_op jit(solution)/shard_map/dot_general | solution.py:53
  126.8 3.0 %all-to-all-done.2 = f32[16,34,896]{2,1,0:T(8,128)} async-done(((f32[16,34,896]{2,1,0:T(8,128)}), f32[16,34,896]{2,1,0:T(8,128)}, u32[]{:S(2)}, u32[]{:S(2)}) %all-to-all-start.2) | async-done | bytes 1949728 | tf_op jit(solution)/shard_map/all_to_all | solution.py:45
  129.7 9.8 %all-to-all-start.3 = ((f32[8,136,576]{2,1,0:T(8,128)}), f32[8,136,576]{2,1,0:T(8,128)}, u32[]{:S(2)}, u32[]{:S(2)}) async-start(f32[8,136,576]{2,1,0:T(8,128)} %bitcast.25), calls=%async_computation.3 | async-start | bytes 5570560 | tf_op jit(solution)/shard_map/all_to_all | solution.py:37
  139.5 0.0 all-gather.5.cloned.1.call-start
  139.6 2.4 reduce_sum.28
  142.0 0.0 all-gather.5.cloned.1.call-update
  142.0 33.7 %all-to-all-done.3 = f32[8,136,576]{2,1,0:T(8,128)} async-done(((f32[8,136,576]{2,1,0:T(8,128)}), f32[8,136,576]{2,1,0:T(8,128)}, u32[]{:S(2)}, u32[]{:S(2)}) %all-to-all-start.3) | async-done | bytes 2506784 | tf_op jit(solution)/shard_map/all_to_all | solution.py:37
  175.7 1.9 reduce_sum.29
  177.6 1.2 broadcast_in_dim.7
  178.8 4.3 %all-to-all-start.4 = ((bf16[8,136,576]{2,1,0:T(8,128)(2,1)}), bf16[8,136,576]{2,1,0:T(8,128)(2,1)}, u32[]{:S(2)}, u32[]{:S(2)}) async-start(bf16[8,136,576]{2,1,0:T(8,128)(2,1)} %broadcast_in_dim.7), calls=%async_computation.4 | async-start | bytes 2785280 | tf_op jit(solution)/shard_map/all_to_all | solution.py:20
  183.8 20.2 %all-gather.5.cloned.1.call-done = bf16[32,34,896]{2,1,0:T(8,128)(2,1)} async-done(((bf16[1,34,896]{2,1,0:T(8,128)(2,1)}), bf16[32,34,896]{2,1,0:T(8,128)(2,1)}) %all-gather.5.cloned.1.call-update) | async-done | bytes 1949712 | tf_op jit(solution)/shard_map/all_gather | solution.py:67
  204.0 4.0 %reshape.25 = bf16[8,136,896]{2,1,0:T(8,128)(2,1)} reshape(bf16[32,34,896]{2,1,0:T(8,128)(2,1)} %all-gather.5.cloned.1.call-done) | data formatting | bytes 3899392 | tf_op jit(solution)/shard_map/reshape | solution.py:73
  208.0 2.9 %slice.18 = bf16[8,128,896]{2,1,0:T(8,128)(2,1)} slice(bf16[8,136,896]{2,1,0:T(8,128)(2,1)} %reshape.25), slice={[0:8], [0:128], [0:896]} | slice | bytes 3670016 | tf_op jit(solution)/shard_map/slice | solution.py:74
  210.8 0.2 all-to-all-done.4
  211.0 3.5 %reshape_reshape.4 = bf16[32,34,576]{2,1,0:T(8,128)(2,1)} reshape(bf16[8,136,576]{2,1,0:T(8,128)(2,1)} %all-to-all-done.4) | data formatting | bytes 2506752 | tf_op jit(solution)/shard_map/reshape;reshape | solution.py:70
  214.6 1.0 slice.17
  215.6 2.5 slice.19
  218.1 0.1 reshape.28
  218.2 55.0 %while.14 = (s32[]{:T(128)}, f32[896,576]{0,1:T(8,128)}, bf16[1024,896]{1,0:T(8,128)(2,1)}, bf16[1024,576]{1,0:T(8,128)(2,1)}, s32[]{:T(128)}, /*index=5*/s32[]{:T(128)}, s32[]{:T(128)}, s32[]{:T(128)}) while((s32[]{:T(128)}, f32[896,576]{0,1:T(8,128)}, bf16[1024,896]{1,0:T(8,128)(2,1)}, bf16[1024,576]{1,0:T(8,128)(2,1)}, ...), condition=%wide.region_4.0_spmd.clone, body=%wide.region_3.0_spmd.clone.sunk | while | flops 67608584 | bytes 4327060 | solution.py:86
  218.2 2.7 select_add_fusion.2
  220.9 3.5 %select_add_fusion.2 = f32[896,576]{0,1:T(8,128)} fusion(f32[896,576]{0,1:T(8,128)} %get-tuple-element.142, pred[]{:T(512)S(6)} %compare.3, bf16[1024,896]{1,0:T(8,128)(2,1)} %get-tuple-element.151, s32[]{:T(128)S(6)} %select_n.10, bf16[1024,576]{1,0:T(8,128)(2,1)} %get-tuple-element.152), kind=kOutput, calls=%fused_computation.clone.1 | convolution fusion | flops 67608576 | bytes 4326912 | tf_op jit(solution)/shard_map/while/body/eval_jaxpr/dot_general | solution.py:80
  224.4 3.5 %select_add_fusion.2 = f32[896,576]{0,1:T(8,128)} fusion(f32[896,576]{0,1:T(8,128)} %get-tuple-element.142, pred[]{:T(512)S(6)} %compare.3, bf16[1024,896]{1,0:T(8,128)(2,1)} %get-tuple-element.151, s32[]{:T(128)S(6)} %select_n.10, bf16[1024,576]{1,0:T(8,128)(2,1)} %get-tuple-element.152), kind=kOutput, calls=%fused_computation.clone.1 | convolution fusion | flops 67608576 | bytes 4326912 | tf_op jit(solution)/shard_map/while/body/eval_jaxpr/dot_general | solution.py:80
  227.9 3.5 %select_add_fusion.2 = f32[896,576]{0,1:T(8,128)} fusion(f32[896,576]{0,1:T(8,128)} %get-tuple-element.142, pred[]{:T(512)S(6)} %compare.3, bf16[1024,896]{1,0:T(8,128)(2,1)} %get-tuple-element.151, s32[]{:T(128)S(6)} %select_n.10, bf16[1024,576]{1,0:T(8,128)(2,1)} %get-tuple-element.152), kind=kOutput, calls=%fused_computation.clone.1 | convolution fusion | flops 67608576 | bytes 4326912 | tf_op jit(solution)/shard_map/while/body/eval_jaxpr/dot_general | solution.py:80
  231.4 3.5 %select_add_fusion.2 = f32[896,576]{0,1:T(8,128)} fusion(f32[896,576]{0,1:T(8,128)} %get-tuple-element.142, pred[]{:T(512)S(6)} %compare.3, bf16[1024,896]{1,0:T(8,128)(2,1)} %get-tuple-element.151, s32[]{:T(128)S(6)} %select_n.10, bf16[1024,576]{1,0:T(8,128)(2,1)} %get-tuple-element.152), kind=kOutput, calls=%fused_computation.clone.1 | convolution fusion | flops 67608576 | bytes 4326912 | tf_op jit(solution)/shard_map/while/body/eval_jaxpr/dot_general | solution.py:80
  234.9 3.5 %select_add_fusion.2 = f32[896,576]{0,1:T(8,128)} fusion(f32[896,576]{0,1:T(8,128)} %get-tuple-element.142, pred[]{:T(512)S(6)} %compare.3, bf16[1024,896]{1,0:T(8,128)(2,1)} %get-tuple-element.151, s32[]{:T(128)S(6)} %select_n.10, bf16[1024,576]{1,0:T(8,128)(2,1)} %get-tuple-element.152), kind=kOutput, calls=%fused_computation.clone.1 | convolution fusion | flops 67608576 | bytes 4326912 | tf_op jit(solution)/shard_map/while/body/eval_jaxpr/dot_general | solution.py:80
  238.3 3.5 %select_add_fusion.2 = f32[896,576]{0,1:T(8,128)} fusion(f32[896,576]{0,1:T(8,128)} %get-tuple-element.142, pred[]{:T(512)S(6)} %compare.3, bf16[1024,896]{1,0:T(8,128)(2,1)} %get-tuple-element.151, s32[]{:T(128)S(6)} %select_n.10, bf16[1024,576]{1,0:T(8,128)(2,1)} %get-tuple-element.152), kind=kOutput, calls=%fused_computation.clone.1 | convolution fusion | flops 67608576 | bytes 4326912 | tf_op jit(solution)/shard_map/while/body/eval_jaxpr/dot_general | solution.py:80
  241.8 3.5 %select_add_fusion.2 = f32[896,576]{0,1:T(8,128)} fusion(f32[896,576]{0,1:T(8,128)} %get-tuple-element.142, pred[]{:T(512)S(6)} %compare.3, bf16[1024,896]{1,0:T(8,128)(2,1)} %get-tuple-element.151, s32[]{:T(128)S(6)} %select_n.10, bf16[1024,576]{1,0:T(8,128)(2,1)} %get-tuple-element.152), kind=kOutput, calls=%fused_computation.clone.1 | convolution fusion | flops 67608576 | bytes 4326912 | tf_op jit(solution)/shard_map/while/body/eval_jaxpr/dot_general | solution.py:80
  245.3 3.5 %select_add_fusion.2 = f32[896,576]{0,1:T(8,128)} fusion(f32[896,576]{0,1:T(8,128)} %get-tuple-element.142, pred[]{:T(512)S(6)} %compare.3, bf16[1024,896]{1,0:T(8,128)(2,1)} %get-tuple-element.151, s32[]{:T(128)S(6)} %select_n.10, bf16[1024,576]{1,0:T(8,128)(2,1)} %get-tuple-element.152), kind=kOutput, calls=%fused_computation.clone.1 | convolution fusion | flops 67608576 | bytes 4326912 | tf_op jit(solution)/shard_map/while/body/eval_jaxpr/dot_general | solution.py:80
  248.8 3.5 %select_add_fusion.2 = f32[896,576]{0,1:T(8,128)} fusion(f32[896,576]{0,1:T(8,128)} %get-tuple-element.142, pred[]{:T(512)S(6)} %compare.3, bf16[1024,896]{1,0:T(8,128)(2,1)} %get-tuple-element.151, s32[]{:T(128)S(6)} %select_n.10, bf16[1024,576]{1,0:T(8,128)(2,1)} %get-tuple-element.152), kind=kOutput, calls=%fused_computation.clone.1 | convolution fusion | flops 67608576 | bytes 4326912 | tf_op jit(solution)/shard_map/while/body/eval_jaxpr/dot_general | solution.py:80
  252.3 3.5 %select_add_fusion.2 = f32[896,576]{0,1:T(8,128)} fusion(f32[896,576]{0,1:T(8,128)} %get-tuple-element.142, pred[]{:T(512)S(6)} %compare.3, bf16[1024,896]{1,0:T(8,128)(2,1)} %get-tuple-element.151, s32[]{:T(128)S(6)} %select_n.10, bf16[1024,576]{1,0:T(8,128)(2,1)} %get-tuple-element.152), kind=kOutput, calls=%fused_computation.clone.1 | convolution fusion | flops 67608576 | bytes 4326912 | tf_op jit(solution)/shard_map/while/body/eval_jaxpr/dot_general | solution.py:80
  255.8 3.5 %select_add_fusion.2 = f32[896,576]{0,1:T(8,128)} fusion(f32[896,576]{0,1:T(8,128)} %get-tuple-element.142, pred[]{:T(512)S(6)} %compare.3, bf16[1024,896]{1,0:T(8,128)(2,1)} %get-tuple-element.151, s32[]{:T(128)S(6)} %select_n.10, bf16[1024,576]{1,0:T(8,128)(2,1)} %get-tuple-element.152), kind=kOutput, calls=%fused_computation.clone.1 | convolution fusion | flops 67608576 | bytes 4326912 | tf_op jit(solution)/shard_map/while/body/eval_jaxpr/dot_general | solution.py:80
  259.2 3.5 %select_add_fusion.2 = f32[896,576]{0,1:T(8,128)} fusion(f32[896,576]{0,1:T(8,128)} %get-tuple-element.142, pred[]{:T(512)S(6)} %compare.3, bf16[1024,896]{1,0:T(8,128)(2,1)} %get-tuple-element.151, s32[]{:T(128)S(6)} %select_n.10, bf16[1024,576]{1,0:T(8,128)(2,1)} %get-tuple-element.152), kind=kOutput, calls=%fused_computation.clone.1 | convolution fusion | flops 67608576 | bytes 4326912 | tf_op jit(solution)/shard_map/while/body/eval_jaxpr/dot_general | solution.py:80
  262.7 3.5 %select_add_fusion.2 = f32[896,576]{0,1:T(8,128)} fusion(f32[896,576]{0,1:T(8,128)} %get-tuple-element.142, pred[]{:T(512)S(6)} %compare.3, bf16[1024,896]{1,0:T(8,128)(2,1)} %get-tuple-element.151, s32[]{:T(128)S(6)} %select_n.10, bf16[1024,576]{1,0:T(8,128)(2,1)} %get-tuple-element.152), kind=kOutput, calls=%fused_computation.clone.1 | convolution fusion | flops 67608576 | bytes 4326912 | tf_op jit(solution)/shard_map/while/body/eval_jaxpr/dot_general | solution.py:80
  266.2 3.5 %select_add_fusion.2 = f32[896,576]{0,1:T(8,128)} fusion(f32[896,576]{0,1:T(8,128)} %get-tuple-element.142, pred[]{:T(512)S(6)} %compare.3, bf16[1024,896]{1,0:T(8,128)(2,1)} %get-tuple-element.151, s32[]{:T(128)S(6)} %select_n.10, bf16[1024,576]{1,0:T(8,128)(2,1)} %get-tuple-element.152), kind=kOutput, calls=%fused_computation.clone.1 | convolution fusion | flops 67608576 | bytes 4326912 | tf_op jit(solution)/shard_map/while/body/eval_jaxpr/dot_general | solution.py:80
  269.7 3.5 %select_add_fusion.2 = f32[896,576]{0,1:T(8,128)} fusion(f32[896,576]{0,1:T(8,128)} %get-tuple-element.142, pred[]{:T(512)S(6)} %compare.3, bf16[1024,896]{1,0:T(8,128)(2,1)} %get-tuple-element.151, s32[]{:T(128)S(6)} %select_n.10, bf16[1024,576]{1,0:T(8,128)(2,1)} %get-tuple-element.152), kind=kOutput, calls=%fused_computation.clone.1 | convolution fusion | flops 67608576 | bytes 4326912 | tf_op jit(solution)/shard_map/while/body/eval_jaxpr/dot_general | solution.py:80
  273.2 3.4 %add_divide_fusion = f32[896,576]{0,1:T(8,128)} fusion(f32[896,576]{0,1:T(8,128)} %get-tuple-element.84, bf16[64,576]{1,0:T(8,128)(2,1)S(1)} %reshape.28, f32[]{:T(128)} %bitcast.23, bf16[8,136,896]{2,1,0:T(8,128)(2,1)} %reshape.25), kind=kOutput, calls=%fused_computation.5 | convolution fusion | flops 67608576 | bytes 4317696 | tf_op jit(solution)/shard_map/dot_general | solution.py:89
  (2 shorter events, 0.0 us)
Async XLA Ops:
  6.5 112.2 %copy-start = (bf16[2304,576]{0,1:T(8,128)(2,1)S(1)}, bf16[2304,576]{0,1:T(8,128)(2,1)}, u32[]{:S(2)}) copy-start(bf16[2304,576]{0,1:T(8,128)(2,1)} %param.13) | copy-start | bytes 7962628
  6.5 104.4 %all-gather.7.cloned.1.call-start = ((), (), s32[]{:S(2)}) async-start(), calls=%async_computation.6 | async-start | bytes 6082560 | tf_op jit(solution)/shard_map/all_gather | solution.py:54
  47.4 82.3 %all-to-all-start.2 = ((f32[16,34,896]{2,1,0:T(8,128)}), f32[16,34,896]{2,1,0:T(8,128)}, u32[]{:S(2)}, u32[]{:S(2)}) async-start(f32[16,34,896]{2,1,0:T(8,128)} %copy.24), calls=%async_computation.2 | async-start | bytes 4587520 | tf_op jit(solution)/shard_map/all_to_all | solution.py:45
  129.7 45.9 %all-to-all-start.3 = ((f32[8,136,576]{2,1,0:T(8,128)}), f32[8,136,576]{2,1,0:T(8,128)}, u32[]{:S(2)}, u32[]{:S(2)}) async-start(f32[8,136,576]{2,1,0:T(8,128)} %bitcast.25), calls=%async_computation.3 | async-start | bytes 5570560 | tf_op jit(solution)/shard_map/all_to_all | solution.py:37
  139.5 64.4 %all-gather.5.cloned.1.call-start = ((), (), s32[]{:S(2)}) async-start(), calls=%async_computation.5 | async-start | bytes 2365440 | tf_op jit(solution)/shard_map/all_gather | solution.py:67
  178.8 32.2 %all-to-all-start.4 = ((bf16[8,136,576]{2,1,0:T(8,128)(2,1)}), bf16[8,136,576]{2,1,0:T(8,128)(2,1)}, u32[]{:S(2)}, u32[]{:S(2)}) async-start(bf16[8,136,576]{2,1,0:T(8,128)(2,1)} %broadcast_in_dim.7), calls=%async_computation.4 | async-start | bytes 2785280 | tf_op jit(solution)/shard_map/all_to_all | solution.py:20
Sparse Core Ops, SparseCore 0:
  10.0 100.9 all-gather.6
  142.9 61.0 all-gather.4
where the time goes:
time: 285 us; the launch traced here: 283 us
  waiting for transfers between devices  111 us (39%)
  matrix products  68.3 us (24%)
  local copies, waits for them, and re-layouts  30.1 us (11%)
  blocking collectives  25.4 us (9%)
  starting transfers between devices  24 us (8%)
  between operations  14.1 us (5%)
  other arithmetic  10.8 us (4%)
    dot_general x16, matrix products, accumulate(): lax.dot_general(grad_block, act_block, (((0,), (0,)), ((), ())), preferre...  55 us
    all_gather x1, waiting for transfers between devices, shards(): lax.all_gather(act_local, ROW, axis=0, tiled=True)  53.6 us
    all_to_all x1, waiting for transfers between devices, sent_and_summed(): lax.all_to_all(tiles, axis, split_axis=0, concat_axis=0, tiled=True)  33.7 us
    all_gather x1, waiting for transfers between devices, shards(): summed_out = lax.all_gather(share_out, ROW, axis=0, tiled=True)  20.2 us
    all_to_all x1, blocking collectives, copy_for_each(): lax.all_to_all(jnp.broadcast_to(value[None], (peers, *value.shape)), axis...  15.6 us
    all_to_all x1, starting transfers between devices, summed_rows(): lax.all_to_all(nearer, far, split_axis=0, concat_axis=0, tiled=True)  9.91 us
    all_to_all x1, starting transfers between devices, sent_and_summed(): lax.all_to_all(tiles, axis, split_axis=0, concat_axis=0, tiled=True)  9.8 us
    all_to_all x1, blocking collectives, sent_and_summed(): lax.all_to_all(tiles, axis, split_axis=0, concat_axis=0, tiled=True)  9.74 us
  transfers between devices with their start and end apart: 5, of which 5 were waited for; matrix products, arithmetic and copies ran while one was open for 15% of the time, Pallas kernels for 0%

commit v1 on v0

--- a/solution.py
+++ b/solution.py
@@ -64,7 +64,9 @@
     share_in = sent_and_summed(partial_in, "col", 0).astype(jnp.bfloat16)
     summed_in = gathered_copies(share_in, "col", 0)
     share_out = summed_rows(partial_out, (("row_0", "row_1"), "row_2"), 0).astype(jnp.bfloat16)
-    summed_out = lax.all_gather(share_out, ROW, axis=0, tiled=True)
+    summed_out = jnp.concatenate(
+        lax.all_to_all(jnp.stack([share_out] * lax.axis_size(ROW)), ROW, 0, 0), axis=0
+    )
     width_in = summed_in.shape[1]
     width_out = summed_out.shape[1]
     groups_in = summed_in.reshape(lax.axis_size(ROW), block_act, width_in)

time: 285 us -> 342 us (1.20)
  waiting for transfers between devices: 111 us -> 154 us
  starting transfers between devices: 24 us -> 36.8 us
    all_to_all x0 -> x1, waiting for transfers between devices: none -> 54.2 us  [shards(): lax.all_to_all(jnp.stack([share_out] * lax.axis_size(ROW)), ROW, 0, 0)]
    all_gather x1 -> x0, waiting for transfers between devices: 20.2 us -> none  [shards(): summed_out = lax.all_gather(share_out, ROW, axis=0, tiled=True)]
    all_to_all x0 -> x1, starting transfers between devices: none -> 12.8 us  [shards(): lax.all_to_all(jnp.stack([share_out] * lax.axis_size(ROW)), ROW, 0, 0)]
    all_to_all x1, waiting for transfers between devices: 0.19 us -> 10.8 us  [copy_for_each(): lax.all_to_all(jnp.broadcast_to(value[None], (peers, *value.shape)), axis...]
    another operation x0 -> x2, local copies, waits for them, and re-layouts: none -> 5.59 us  [the longest x1 4 us: shards(): groups_out = summed_out.reshape(lax.axis_size('col'), block_grad, width_out)]
    reshape x1 -> x0, local copies, waits for them, and re-layouts: 3.99 us -> none  [shards(): groups_out = summed_out.reshape(lax.axis_size('col'), block_grad, width_out)]
  transfers between devices with their start and end apart: 5 -> 5, of which waited for: 5 -> 5; matrix products, arithmetic and copies ran while one was open for 15% -> 12% of each run, Pallas kernels for 0% -> 0%
where the time goes in v1:
time: 342 us; the launch traced here: 340 us
  waiting for transfers between devices  154 us (45%)
  matrix products  68.4 us (20%)
  starting transfers between devices  36.8 us (11%)
  local copies, waits for them, and re-layouts  31.7 us (9%)
  blocking collectives  25.4 us (7%)
  between operations  14.1 us (4%)
  other arithmetic  10.1 us (3%)
    dot_general x16, matrix products, accumulate(): lax.dot_general(grad_block, act_block, (((0,), (0,)), ((), ())), preferre...  55 us
    all_to_all x1, waiting for transfers between devices, shards(): lax.all_to_all(jnp.stack([share_out] * lax.axis_size(ROW)), ROW, 0, 0)  54.2 us
    all_gather x1, waiting for transfers between devices, shards(): lax.all_gather(act_local, ROW, axis=0, tiled=True)  53.6 us
    all_to_all x1, waiting for transfers between devices, sent_and_summed(): lax.all_to_all(tiles, axis, split_axis=0, concat_axis=0, tiled=True)  32.3 us
    all_to_all x1, blocking collectives, copy_for_each(): lax.all_to_all(jnp.broadcast_to(value[None], (peers, *value.shape)), axis...  15.6 us
    all_to_all x1, starting transfers between devices, shards(): lax.all_to_all(jnp.stack([share_out] * lax.axis_size(ROW)), ROW, 0, 0)  12.8 us
    all_to_all x1, waiting for transfers between devices, copy_for_each(): lax.all_to_all(jnp.broadcast_to(value[None], (peers, *value.shape)), axis...  10.8 us
    all_to_all x1, starting transfers between devices, summed_rows(): lax.all_to_all(nearer, far, split_axis=0, concat_axis=0, tiled=True)  9.89 us
  transfers between devices with their start and end apart: 5, of which 5 were waited for; matrix products, arithmetic and copies ran while one was open for 12% of the time, Pallas kernels for 0%

profile of v1, /device:TPU:1, one launch (start us, length us, event | category | flops | bytes accessed | tf_op | source)
XLA Modules:
  0.0 340.4 jit_solution(14963299057510112352)
XLA Ops:
  6.5 0.0 copy-start
  6.5 0.0 all-gather.3.cloned.1.call-start
  6.5 1.8 maximum_bitcast_fusion
  8.3 0.0 all-gather.3.cloned.1.call-update
  8.3 0.8 copy.21
  9.2 0.8 pad_maximum_fusion
  10.0 0.1 copy.22
  10.2 15.6 %all_to_all.30 = bf16[8,136,224]{2,1,0:T(8,128)(2,1)} all-to-all(bf16[8,136,224]{2,1,0:T(8,128)(2,1)S(1)} %broadcast_in_dim.6), channel_id=1, replica_groups=mesh['row_0'=4,'row_1'=4,'row_2'=2,'col'=8] {'col'}, dimensions={0} | all-to-all | bytes 974848 | tf_op jit(solution)/shard_map/all_to_all | solution.py:20
  25.8 1.4 dot_general.18
  27.2 1.9 convolution_bitcast_fusion
  29.0 1.3 copy.23
  30.3 9.8 %all_to_all.31 = f32[2,16,34,896]{3,1,2,0:T(8,128)} all-to-all(f32[2,16,34,896]{3,1,2,0:T(8,128)S(1)} %copy.23), channel_id=1, replica_groups=mesh['row_0'=4,'row_1'=4,'row_2'=2,'col'=8] {'row_2'}, dimensions={0} | all-to-all | bytes 7798784 | tf_op jit(solution)/shard_map/all_to_all | solution.py:37
  40.0 3.8 %reduce_sum.27 = f32[16,34,896]{2,0,1:T(8,128)} reduce(f32[2,16,34,896]{3,1,2,0:T(8,128)} %all_to_all.31, f32[]{:T(128)} %constant.33.clone.1), dimensions={0}, to_apply=%region_0.0 | reduce | flops 487424 | bytes 5849092 | tf_op jit(solution)/shard_map/reduce_sum | solution.py:38
  43.9 3.5 %copy.24 = f32[16,34,896]{2,1,0:T(8,128)} copy(f32[16,34,896]{2,0,1:T(8,128)} %reduce_sum.27) | data formatting | bytes 3899392 | tf_op jit(solution)/shard_map/reduce_sum | solution.py:38
  47.4 9.9 %all-to-all-start.2 = ((f32[16,34,896]{2,1,0:T(8,128)}), f32[16,34,896]{2,1,0:T(8,128)}, u32[]{:S(2)}, u32[]{:S(2)}) async-start(f32[16,34,896]{2,1,0:T(8,128)} %copy.24), calls=%async_computation.2 | async-start | bytes 4587520 | tf_op jit(solution)/shard_map/all_to_all | solution.py:45
  57.3 53.6 %all-gather.3.cloned.1.call-done = bf16[32,34,2304]{2,1,0:T(8,128)(2,1)} async-done(((bf16[1,34,2304]{2,1,0:T(8,128)(2,1)}), bf16[32,34,2304]{2,1,0:T(8,128)(2,1)}) %all-gather.3.cloned.1.call-update) | async-done | bytes 5013520 | tf_op jit(solution)/shard_map/all_gather | solution.py:54
  110.9 7.7 %reshape.30 = bf16[1088,2304]{1,0:T(8,128)(2,1)} reshape(bf16[32,34,2304]{2,1,0:T(8,128)(2,1)} %all-gather.3.cloned.1.call-done) | data formatting | bytes 10027008
  118.7 0.0 copy-done
  118.7 8.1 %fusion.4 = f32[1088,576]{1,0:T(8,128)} fusion(bf16[1088,2304]{1,0:T(8,128)(2,1)} %reshape.30, bf16[2304,576]{0,1:T(8,128)(2,1)S(1)} %copy-done), kind=kOutput, calls=%fused_computation.10 | convolution fusion | flops 2887778304 | bytes 10174464 | tf_op jit(solution)/shard_map/dot_general | solution.py:53
  126.8 2.9 all-to-all-done.2
  129.7 9.8 %all-to-all-start.4 = ((f32[8,136,576]{2,1,0:T(8,128)}), f32[8,136,576]{2,1,0:T(8,128)}, u32[]{:S(2)}, u32[]{:S(2)}) async-start(f32[8,136,576]{2,1,0:T(8,128)} %bitcast.22), calls=%async_computation.4 | async-start | bytes 5570560 | tf_op jit(solution)/shard_map/all_to_all | solution.py:37
  139.6 1.8 reduce_sum.28
  141.3 32.3 %all-to-all-done.4 = f32[8,136,576]{2,1,0:T(8,128)} async-done(((f32[8,136,576]{2,1,0:T(8,128)}), f32[8,136,576]{2,1,0:T(8,128)}, u32[]{:S(2)}, u32[]{:S(2)}) %all-to-all-start.4) | async-done | bytes 2506784 | tf_op jit(solution)/shard_map/all_to_all | solution.py:37
  173.6 1.6 stack.2
  175.2 12.8 %all-to-all-start.3 = ((bf16[32,34,896]{2,1,0:T(8,128)(2,1)}), bf16[32,34,896]{2,1,0:T(8,128)(2,1)}, u32[]{:S(2)}, u32[]{:S(2)}) async-start(bf16[32,34,896]{2,1,0:T(8,128)(2,1)} %stack.2), calls=%async_computation.3 | async-start | bytes 4587520 | tf_op jit(solution)/shard_map/all_to_all | solution.py:68
  188.0 1.9 reduce_sum.29
  190.0 54.2 %all-to-all-done.3 = bf16[32,34,896]{2,1,0:T(8,128)(2,1)} async-done(((bf16[32,34,896]{2,1,0:T(8,128)(2,1)}), bf16[32,34,896]{2,1,0:T(8,128)(2,1)}, u32[]{:S(2)}, u32[]{:S(2)}) %all-to-all-start.3) | async-done | bytes 1949728 | tf_op jit(solution)/shard_map/all_to_all | solution.py:68
  244.1 1.2 broadcast_in_dim.7
  245.3 4.3 %all-to-all-start.5 = ((bf16[8,136,576]{2,1,0:T(8,128)(2,1)}), bf16[8,136,576]{2,1,0:T(8,128)(2,1)}, u32[]{:S(2)}, u32[]{:S(2)}) async-start(bf16[8,136,576]{2,1,0:T(8,128)(2,1)} %broadcast_in_dim.7), calls=%async_computation.5 | async-start | bytes 2785280 | tf_op jit(solution)/shard_map/all_to_all | solution.py:20
  250.3 4.0 %reshape_reshape.7 = bf16[8,136,896]{2,1,0:T(8,128)(2,1)} reshape(bf16[32,34,896]{2,1,0:T(8,128)(2,1)} %all-to-all-done.3) | data formatting | bytes 3899392 | tf_op jit(solution)/shard_map/reshape;reshape | solution.py:75
  254.3 2.9 slice.18
  257.2 10.8 %all-to-all-done.5 = bf16[8,136,576]{2,1,0:T(8,128)(2,1)} async-done(((bf16[8,136,576]{2,1,0:T(8,128)(2,1)}), bf16[8,136,576]{2,1,0:T(8,128)(2,1)}, u32[]{:S(2)}, u32[]{:S(2)}) %all-to-all-start.5) | async-done | bytes 1253408 | tf_op jit(solution)/shard_map/all_to_all | solution.py:20
  267.9 3.5 %reshape_reshape.8 = bf16[32,34,576]{2,1,0:T(8,128)(2,1)} reshape(bf16[8,136,576]{2,1,0:T(8,128)(2,1)} %all-to-all-done.5) | data formatting | bytes 2506752 | tf_op jit(solution)/shard_map/reshape;reshape | solution.py:72
  271.5 1.0 slice.17
  272.5 2.5 slice.19
  275.0 0.1 reshape.26
  275.1 55.0 %while.14 = (s32[]{:T(128)}, f32[896,576]{0,1:T(8,128)}, bf16[1024,896]{1,0:T(8,128)(2,1)}, bf16[1024,576]{1,0:T(8,128)(2,1)}, s32[]{:T(128)}, /*index=5*/s32[]{:T(128)}, s32[]{:T(128)}, s32[]{:T(128)}) while((s32[]{:T(128)}, f32[896,576]{0,1:T(8,128)}, bf16[1024,896]{1,0:T(8,128)(2,1)}, bf16[1024,576]{1,0:T(8,128)(2,1)}, ...), condition=%wide.region_4.0_spmd.clone, body=%wide.region_3.0_spmd.clone.sunk | while | flops 67608584 | bytes 4327060 | solution.py:88
  275.1 2.7 select_add_fusion.2
  277.9 3.5 %select_add_fusion.2 = f32[896,576]{0,1:T(8,128)} fusion(f32[896,576]{0,1:T(8,128)} %get-tuple-element.142, pred[]{:T(512)S(6)} %compare.3, bf16[1024,896]{1,0:T(8,128)(2,1)} %get-tuple-element.151, s32[]{:T(128)S(6)} %select_n.10, bf16[1024,576]{1,0:T(8,128)(2,1)} %get-tuple-element.152), kind=kOutput, calls=%fused_computation.clone.1 | convolution fusion | flops 67608576 | bytes 4326912 | tf_op jit(solution)/shard_map/while/body/eval_jaxpr/dot_general | solution.py:82
  281.3 3.5 %select_add_fusion.2 = f32[896,576]{0,1:T(8,128)} fusion(f32[896,576]{0,1:T(8,128)} %get-tuple-element.142, pred[]{:T(512)S(6)} %compare.3, bf16[1024,896]{1,0:T(8,128)(2,1)} %get-tuple-element.151, s32[]{:T(128)S(6)} %select_n.10, bf16[1024,576]{1,0:T(8,128)(2,1)} %get-tuple-element.152), kind=kOutput, calls=%fused_computation.clone.1 | convolution fusion | flops 67608576 | bytes 4326912 | tf_op jit(solution)/shard_map/while/body/eval_jaxpr/dot_general | solution.py:82
  284.8 3.5 %select_add_fusion.2 = f32[896,576]{0,1:T(8,128)} fusion(f32[896,576]{0,1:T(8,128)} %get-tuple-element.142, pred[]{:T(512)S(6)} %compare.3, bf16[1024,896]{1,0:T(8,128)(2,1)} %get-tuple-element.151, s32[]{:T(128)S(6)} %select_n.10, bf16[1024,576]{1,0:T(8,128)(2,1)} %get-tuple-element.152), kind=kOutput, calls=%fused_computation.clone.1 | convolution fusion | flops 67608576 | bytes 4326912 | tf_op jit(solution)/shard_map/while/body/eval_jaxpr/dot_general | solution.py:82
  288.3 3.5 %select_add_fusion.2 = f32[896,576]{0,1:T(8,128)} fusion(f32[896,576]{0,1:T(8,128)} %get-tuple-element.142, pred[]{:T(512)S(6)} %compare.3, bf16[1024,896]{1,0:T(8,128)(2,1)} %get-tuple-element.151, s32[]{:T(128)S(6)} %select_n.10, bf16[1024,576]{1,0:T(8,128)(2,1)} %get-tuple-element.152), kind=kOutput, calls=%fused_computation.clone.1 | convolution fusion | flops 67608576 | bytes 4326912 | tf_op jit(solution)/shard_map/while/body/eval_jaxpr/dot_general | solution.py:82
  291.8 3.5 %select_add_fusion.2 = f32[896,576]{0,1:T(8,128)} fusion(f32[896,576]{0,1:T(8,128)} %get-tuple-element.142, pred[]{:T(512)S(6)} %compare.3, bf16[1024,896]{1,0:T(8,128)(2,1)} %get-tuple-element.151, s32[]{:T(128)S(6)} %select_n.10, bf16[1024,576]{1,0:T(8,128)(2,1)} %get-tuple-element.152), kind=kOutput, calls=%fused_computation.clone.1 | convolution fusion | flops 67608576 | bytes 4326912 | tf_op jit(solution)/shard_map/while/body/eval_jaxpr/dot_general | solution.py:82
  295.3 3.5 %select_add_fusion.2 = f32[896,576]{0,1:T(8,128)} fusion(f32[896,576]{0,1:T(8,128)} %get-tuple-element.142, pred[]{:T(512)S(6)} %compare.3, bf16[1024,896]{1,0:T(8,128)(2,1)} %get-tuple-element.151, s32[]{:T(128)S(6)} %select_n.10, bf16[1024,576]{1,0:T(8,128)(2,1)} %get-tuple-element.152), kind=kOutput, calls=%fused_computation.clone.1 | convolution fusion | flops 67608576 | bytes 4326912 | tf_op jit(solution)/shard_map/while/body/eval_jaxpr/dot_general | solution.py:82
  298.7 3.5 %select_add_fusion.2 = f32[896,576]{0,1:T(8,128)} fusion(f32[896,576]{0,1:T(8,128)} %get-tuple-element.142, pred[]{:T(512)S(6)} %compare.3, bf16[1024,896]{1,0:T(8,128)(2,1)} %get-tuple-element.151, s32[]{:T(128)S(6)} %select_n.10, bf16[1024,576]{1,0:T(8,128)(2,1)} %get-tuple-element.152), kind=kOutput, calls=%fused_computation.clone.1 | convolution fusion | flops 67608576 | bytes 4326912 | tf_op jit(solution)/shard_map/while/body/eval_jaxpr/dot_general | solution.py:82
  302.2 3.5 %select_add_fusion.2 = f32[896,576]{0,1:T(8,128)} fusion(f32[896,576]{0,1:T(8,128)} %get-tuple-element.142, pred[]{:T(512)S(6)} %compare.3, bf16[1024,896]{1,0:T(8,128)(2,1)} %get-tuple-element.151, s32[]{:T(128)S(6)} %select_n.10, bf16[1024,576]{1,0:T(8,128)(2,1)} %get-tuple-element.152), kind=kOutput, calls=%fused_computation.clone.1 | convolution fusion | flops 67608576 | bytes 4326912 | tf_op jit(solution)/shard_map/while/body/eval_jaxpr/dot_general | solution.py:82
  305.7 3.5 %select_add_fusion.2 = f32[896,576]{0,1:T(8,128)} fusion(f32[896,576]{0,1:T(8,128)} %get-tuple-element.142, pred[]{:T(512)S(6)} %compare.3, bf16[1024,896]{1,0:T(8,128)(2,1)} %get-tuple-element.151, s32[]{:T(128)S(6)} %select_n.10, bf16[1024,576]{1,0:T(8,128)(2,1)} %get-tuple-element.152), kind=kOutput, calls=%fused_computation.clone.1 | convolution fusion | flops 67608576 | bytes 4326912 | tf_op jit(solution)/shard_map/while/body/eval_jaxpr/dot_general | solution.py:82
  309.2 3.5 %select_add_fusion.2 = f32[896,576]{0,1:T(8,128)} fusion(f32[896,576]{0,1:T(8,128)} %get-tuple-element.142, pred[]{:T(512)S(6)} %compare.3, bf16[1024,896]{1,0:T(8,128)(2,1)} %get-tuple-element.151, s32[]{:T(128)S(6)} %select_n.10, bf16[1024,576]{1,0:T(8,128)(2,1)} %get-tuple-element.152), kind=kOutput, calls=%fused_computation.clone.1 | convolution fusion | flops 67608576 | bytes 4326912 | tf_op jit(solution)/shard_map/while/body/eval_jaxpr/dot_general | solution.py:82
  312.7 3.5 %select_add_fusion.2 = f32[896,576]{0,1:T(8,128)} fusion(f32[896,576]{0,1:T(8,128)} %get-tuple-element.142, pred[]{:T(512)S(6)} %compare.3, bf16[1024,896]{1,0:T(8,128)(2,1)} %get-tuple-element.151, s32[]{:T(128)S(6)} %select_n.10, bf16[1024,576]{1,0:T(8,128)(2,1)} %get-tuple-element.152), kind=kOutput, calls=%fused_computation.clone.1 | convolution fusion | flops 67608576 | bytes 4326912 | tf_op jit(solution)/shard_map/while/body/eval_jaxpr/dot_general | solution.py:82
  316.1 3.5 %select_add_fusion.2 = f32[896,576]{0,1:T(8,128)} fusion(f32[896,576]{0,1:T(8,128)} %get-tuple-element.142, pred[]{:T(512)S(6)} %compare.3, bf16[1024,896]{1,0:T(8,128)(2,1)} %get-tuple-element.151, s32[]{:T(128)S(6)} %select_n.10, bf16[1024,576]{1,0:T(8,128)(2,1)} %get-tuple-element.152), kind=kOutput, calls=%fused_computation.clone.1 | convolution fusion | flops 67608576 | bytes 4326912 | tf_op jit(solution)/shard_map/while/body/eval_jaxpr/dot_general | solution.py:82
  319.6 3.5 %select_add_fusion.2 = f32[896,576]{0,1:T(8,128)} fusion(f32[896,576]{0,1:T(8,128)} %get-tuple-element.142, pred[]{:T(512)S(6)} %compare.3, bf16[1024,896]{1,0:T(8,128)(2,1)} %get-tuple-element.151, s32[]{:T(128)S(6)} %select_n.10, bf16[1024,576]{1,0:T(8,128)(2,1)} %get-tuple-element.152), kind=kOutput, calls=%fused_computation.clone.1 | convolution fusion | flops 67608576 | bytes 4326912 | tf_op jit(solution)/shard_map/while/body/eval_jaxpr/dot_general | solution.py:82
  323.1 3.5 %select_add_fusion.2 = f32[896,576]{0,1:T(8,128)} fusion(f32[896,576]{0,1:T(8,128)} %get-tuple-element.142, pred[]{:T(512)S(6)} %compare.3, bf16[1024,896]{1,0:T(8,128)(2,1)} %get-tuple-element.151, s32[]{:T(128)S(6)} %select_n.10, bf16[1024,576]{1,0:T(8,128)(2,1)} %get-tuple-element.152), kind=kOutput, calls=%fused_computation.clone.1 | convolution fusion | flops 67608576 | bytes 4326912 | tf_op jit(solution)/shard_map/while/body/eval_jaxpr/dot_general | solution.py:82
  326.6 3.5 %select_add_fusion.2 = f32[896,576]{0,1:T(8,128)} fusion(f32[896,576]{0,1:T(8,128)} %get-tuple-element.142, pred[]{:T(512)S(6)} %compare.3, bf16[1024,896]{1,0:T(8,128)(2,1)} %get-tuple-element.151, s32[]{:T(128)S(6)} %select_n.10, bf16[1024,576]{1,0:T(8,128)(2,1)} %get-tuple-element.152), kind=kOutput, calls=%fused_computation.clone.1 | convolution fusion | flops 67608576 | bytes 4326912 | tf_op jit(solution)/shard_map/while/body/eval_jaxpr/dot_general | solution.py:82
  330.1 3.4 %add_divide_fusion = f32[896,576]{0,1:T(8,128)} fusion(f32[896,576]{0,1:T(8,128)} %get-tuple-element.84, bf16[64,576]{1,0:T(8,128)(2,1)S(1)} %reshape.26, f32[]{:T(128)} %bitcast.20, bf16[8,136,896]{2,1,0:T(8,128)(2,1)} %reshape_reshape.7), kind=kOutput, calls=%fused_computation.5 | convolution fusion | flops 67608576 | bytes 4317696 | tf_op jit(solution)/shard_map/dot_general | solution.py:91
  (2 shorter events, 0.0 us)
Async XLA Ops:
  6.5 112.1 %copy-start = (bf16[2304,576]{0,1:T(8,128)(2,1)S(1)}, bf16[2304,576]{0,1:T(8,128)(2,1)}, u32[]{:S(2)}) copy-start(bf16[2304,576]{0,1:T(8,128)(2,1)} %param.13) | copy-start | bytes 7962628
  6.5 104.4 %all-gather.3.cloned.1.call-start = ((), (), s32[]{:S(2)}) async-start(), calls=%async_computation.6 | async-start | bytes 6082560 | tf_op jit(solution)/shard_map/all_gather | solution.py:54
  47.4 82.3 %all-to-all-start.2 = ((f32[16,34,896]{2,1,0:T(8,128)}), f32[16,34,896]{2,1,0:T(8,128)}, u32[]{:S(2)}, u32[]{:S(2)}) async-start(f32[16,34,896]{2,1,0:T(8,128)} %copy.24), calls=%async_computation.2 | async-start | bytes 4587520 | tf_op jit(solution)/shard_map/all_to_all | solution.py:45
  129.7 43.8 %all-to-all-start.4 = ((f32[8,136,576]{2,1,0:T(8,128)}), f32[8,136,576]{2,1,0:T(8,128)}, u32[]{:S(2)}, u32[]{:S(2)}) async-start(f32[8,136,576]{2,1,0:T(8,128)} %bitcast.22), calls=%async_computation.4 | async-start | bytes 5570560 | tf_op jit(solution)/shard_map/all_to_all | solution.py:37
  175.2 68.9 %all-to-all-start.3 = ((bf16[32,34,896]{2,1,0:T(8,128)(2,1)}), bf16[32,34,896]{2,1,0:T(8,128)(2,1)}, u32[]{:S(2)}, u32[]{:S(2)}) async-start(bf16[32,34,896]{2,1,0:T(8,128)(2,1)} %stack.2), calls=%async_computation.3 | async-start | bytes 4587520 | tf_op jit(solution)/shard_map/all_to_all | solution.py:68
  245.3 22.6 %all-to-all-start.5 = ((bf16[8,136,576]{2,1,0:T(8,128)(2,1)}), bf16[8,136,576]{2,1,0:T(8,128)(2,1)}, u32[]{:S(2)}, u32[]{:S(2)}) async-start(bf16[8,136,576]{2,1,0:T(8,128)(2,1)} %broadcast_in_dim.7), calls=%async_computation.5 | async-start | bytes 2785280 | tf_op jit(solution)/shard_map/all_to_all | solution.py:20
Sparse Core Ops, SparseCore 0:
  10.0 100.9 all-gather.2
